TPU v7x, 256 devices: a whole 4x4x8 slice. The times are simulated.
256 devices in a mesh: blk: 64 (over z_lo, y, x), uly: 4 (over z_hi, core).
Axes of the slice: x: 4, y: 4, z: 8 (z_hi: 2, z_lo: 4; z = z_hi * 4 + z_lo), core: 2. Of those that a mesh axis runs over, the one named last changes fastest.
Arguments:
- video_q: bfloat16 [16384, 3072], P(('blk', 'uly')), may hold values from -6 to 6
- video_k: bfloat16 [16384, 3072], P(('blk', 'uly')), may hold values from -7 to 7
- video_v: bfloat16 [16384, 3072], P(('blk', 'uly')), may hold values from -6 to 6
- text_q: bfloat16 [256, 3072], P('blk', 'uly'), may hold values from -6 to 6
- text_k: bfloat16 [256, 3072], P('blk', 'uly'), may hold values from -6 to 6
- text_v: bfloat16 [256, 3072], P('blk', 'uly'), may hold values from -6 to 6
- video_q_gain: float32 [128], replicated, may hold values from 0.7 to 4, as said below
- video_k_gain: float32 [128], replicated, may hold values from 0.7 to 4, as said below
- text_q_gain: float32 [128], replicated, may hold values from 0.7 to 4, as said below
- text_k_gain: float32 [128], replicated, may hold values from 0.7 to 4, as said below
- frame_ids: int32 [16384], P(('blk', 'uly')), may hold values from 0 to 32, as said below
- row_ids: int32 [16384], P(('blk', 'uly')), may hold values from 0 to 44, as said below
- col_ids: int32 [16384], P(('blk', 'uly')), may hold values from 0 to 79, as said below
- text_mask: int32 [256], P('blk'), may hold values from 0 to 1, as said below
Outputs:
- video_out: bfloat16 [16384, 3072], P(('blk', 'uly'))
- text_out: bfloat16 [256, 3072], P('blk', 'uly')
Inputs may be any that keep to these rules, and one draw needn't show every extreme that they name: `video_q_gain`: positive gains. `video_k_gain`: positive gains. `text_q_gain`: positive gains. `text_k_gain`: positive gains. `frame_ids`: each token's (frame, row, column) is one cell of a clip of 33 frames of 45 x 80 cells, different for every token; every frame holds some tokens. `row_ids`: see frame_ids. `col_ids`: see frame_ids. `text_mask`: a leading run of ones of 64 or more tokens, then zeros, at least one zero.
All inputs are finite; a program needn't handle non-finite values.
Results may differ from a plain program's by a relative error of at most 0.0085.
The roundings to bfloat16 on the way count: a program that leaves them out, or rounds other values in their place, can miss the bound.
Values may be sent and summed in bfloat16 or wider, within the bound.
No kernel may reach another device: no remote copies, remote signals or barrier semaphores. Data moves between devices by JAX's collectives and lax.ppermute only.
A program may use at most 192 MiB of HBM per device.

v0:
```python
import jax
import jax.numpy as jnp
from jax import lax
from jax.sharding import PartitionSpec as P

HD = 128
RT = 16
RH = 56
RW = 56


def rotary_tables(frames, rows_pos, cols_pos):
    angles = []
    for width, position in ((RT, frames), (RH, rows_pos), (RW, cols_pos)):
        index = jnp.arange(width // 2).astype(jnp.float32)
        freqs = jnp.power(jnp.float32(256.0), -2.0 * index / width)
        angles.append(position.astype(jnp.float32)[:, None] * freqs[None, :])
    angle = jnp.concatenate(angles, axis=1)
    return (jnp.cos(angle), jnp.sin(angle))


def norm_heads(values, gain):
    heads_view = values.astype(jnp.float32).reshape(values.shape[0], -1, HD)
    meansq = jnp.mean(heads_view * heads_view, axis=-1, keepdims=True)
    return heads_view * lax.rsqrt(meansq + 1e-06) * gain


def rotate(heads_view, cosine, sine):
    pairs = heads_view.reshape(heads_view.shape[0], heads_view.shape[1], HD // 2, 2)
    first = pairs[..., 0]
    second = pairs[..., 1]
    cos_b = cosine[:, None, :]
    sin_b = sine[:, None, :]
    turned = jnp.stack([first * cos_b - second * sin_b, first * sin_b + second * cos_b], axis=-1)
    return turned.reshape(heads_view.shape[0], -1)


def prepare(values, gain, cosine, sine):
    return rotate(norm_heads(values, gain), cosine, sine).astype(jnp.bfloat16)


def regroup(query_in, key_in, value_in):
    return (
        lax.all_to_all(query_in, "uly", split_axis=1, concat_axis=0, tiled=True),
        lax.all_to_all(key_in, "uly", split_axis=1, concat_axis=0, tiled=True),
        lax.all_to_all(value_in, "uly", split_axis=1, concat_axis=0, tiled=True),
    )


def absorb_block(queries, carry, keys_in, values_in, valid):
    largest, total, accum = carry
    key_heads = keys_in.reshape(keys_in.shape[0], -1, HD)
    value_heads = values_in.reshape(values_in.shape[0], -1, HD)
    scores = jnp.einsum(
        "qhd,khd->hqk", queries, key_heads, preferred_element_type=jnp.float32
    ) / jnp.sqrt(jnp.float32(HD))
    usable = (valid > 0)[None, None, :]
    scores = jnp.where(usable, scores, -1e30)
    newest = jnp.maximum(largest, jnp.max(scores, axis=-1))
    expo = jnp.where(usable, jnp.exp(scores - newest[..., None]), 0.0)
    factor = jnp.exp(largest - newest)
    total = total * factor + jnp.sum(expo, axis=-1)
    accum = accum * factor[..., None] + jnp.einsum(
        "hqk,khd->hqd", expo.astype(jnp.bfloat16), value_heads, preferred_element_type=jnp.float32
    )
    return (newest, total, accum)


def absorb(queries, carry, keys_in, values_in, valid):
    length = keys_in.shape[0]
    blocks = -(-length // 1024)
    while length % blocks != 0:
        blocks = blocks + 1
    if blocks == 1:
        return absorb_block(queries, carry, keys_in, values_in, valid)
    width = length // blocks
    stacked = (
        keys_in.reshape(blocks, width, -1),
        values_in.reshape(blocks, width, -1),
        valid.reshape(blocks, width),
    )

    def advance(state, triple):
        return (absorb_block(queries, state, triple[0], triple[1], triple[2]), None)

    carry, unused = lax.scan(advance, carry, stacked)
    return carry


def body(
    video_q,
    video_k,
    video_v,
    text_q,
    text_k,
    text_v,
    video_q_gain,
    video_k_gain,
    text_q_gain,
    text_k_gain,
    frame_ids,
    row_ids,
    col_ids,
    text_mask,
):
    cosine, sine = rotary_tables(frame_ids, row_ids, col_ids)
    rot_q = prepare(video_q, video_q_gain, cosine, sine)
    rot_k = prepare(video_k, video_k_gain, cosine, sine)
    group_q, group_k, group_v = regroup(rot_q, rot_k, video_v)
    norm_tq = norm_heads(text_q, text_q_gain).astype(jnp.bfloat16).reshape(text_q.shape[0], -1)
    norm_tk = norm_heads(text_k, text_k_gain).astype(jnp.bfloat16).reshape(text_k.shape[0], -1)
    video_rows = group_q.shape[0]
    queries = jnp.concatenate([group_q, norm_tq], axis=0)
    queries = queries.reshape(queries.shape[0], -1, HD)
    head_count = queries.shape[1]
    query_count = queries.shape[0]
    initial = (
        jnp.full((head_count, query_count), -1e30, jnp.float32),
        jnp.zeros((head_count, query_count), jnp.float32),
        jnp.zeros((head_count, query_count, HD), jnp.float32),
    )
    text_keys, text_values, text_valid = (
        lax.all_gather(norm_tk, "blk", axis=0, tiled=True),
        lax.all_gather(text_v, "blk", axis=0, tiled=True),
        lax.all_gather(text_mask, "blk", axis=0, tiled=True),
    )
    carry = absorb(queries, initial, text_keys, text_values, text_valid)
    piece = (
        lax.all_gather(group_k, "blk", axis=0, tiled=True),
        lax.all_gather(group_v, "blk", axis=0, tiled=True),
    )
    filled = jnp.ones((piece[0].shape[0],), jnp.int32)
    carry = absorb(queries, carry, piece[0], piece[1], filled)
    largest, total, accum = carry
    mixed = (accum / total[..., None]).astype(jnp.bfloat16)
    mixed = mixed.transpose(1, 0, 2).reshape(query_count, head_count * HD)
    video_part = mixed[:video_rows]
    text_out = mixed[video_rows:]
    video_out = lax.all_to_all(video_part, "uly", split_axis=0, concat_axis=1, tiled=True)
    return (video_out, text_out)


def solution(mesh):
    in_specs = (
        P(("blk", "uly"), None),
        P(("blk", "uly"), None),
        P(("blk", "uly"), None),
        P("blk", "uly"),
        P("blk", "uly"),
        P("blk", "uly"),
        P(),
        P(),
        P(),
        P(),
        P(("blk", "uly")),
        P(("blk", "uly")),
        P(("blk", "uly")),
        P("blk"),
    )
    out_specs = (P(("blk", "uly"), None), P("blk", "uly"))
    return jax.shard_map(body, mesh=mesh, in_specs=in_specs, out_specs=out_specs, check_vma=False)
```

profile of v0, /device:TPU:1, one launch (start us, length us, event | category | flops | bytes accessed | tf_op | source)
XLA Modules:
  0.0 1055.0 jit_solution(10725916052996982164)
XLA Ops:
  8.4 20.3 %all_to_all.67 = bf16[64,4,768]{2,0,1:T(8,128)(2,1)} all-to-all(bf16[64,4,768]{2,0,1:T(8,128)(2,1)S(1)} %bitcast.97), channel_id=1, replica_groups=mesh['blk'=64,'uly'=4] {'uly'}, dimensions={1} | all-to-all | bytes 786432 | tf_op jit(solution)/shard_map/all_to_all | solution.py:46
  32.5 4.3 subtract_convert_fusion
  36.8 4.2 pad_maximum_fusion
  41.3 17.6 %all_to_all.68 = bf16[64,4,768]{2,0,1:T(8,128)(2,1)} all-to-all(bf16[64,4,768]{2,0,1:T(8,128)(2,1)S(1)} %copy.63), channel_id=1, replica_groups=mesh['blk'=64,'uly'=4] {'uly'}, dimensions={1} | all-to-all | bytes 786432 | tf_op jit(solution)/shard_map/all_to_all | solution.py:45
  60.0 4.9 all-to-all-start
  65.3 172.0 %all-gather = bf16[64,4,768]{2,1,0:T(4,128)(2,1)S(1)} all-gather(bf16[1,4,768]{2,1,0:T(4,128)(2,1)S(1)} %fusion.26), channel_id=1, replica_groups=mesh['blk'=64,'uly'=4] {'blk'}, dimensions={0}, use_global_device_ids=true | all-gather | bytes 399360 | tf_op jit(solution)/shard_map/all_gather | solution.py:123
  237.4 163.5 %all-gather.1 = bf16[64,4,768]{2,1,0:T(4,128)(2,1)S(1)} all-gather(bf16[1,4,768]{2,1,0:T(4,128)(2,1)S(1)} %bitcast.100), channel_id=1, replica_groups=mesh['blk'=64,'uly'=4] {'blk'}, dimensions={0}, use_global_device_ids=true | all-gather | bytes 399360 | tf_op jit(solution)/shard_map/all_gather | solution.py:124
  402.5 11.1 %all-reduce = s32[256]{0:T(256)S(1)} all-reduce(s32[256]{0:T(256)S(1)} %dynamic-update-slice), channel_id=1, replica_groups=mesh['blk'=64,'uly'=4] {'blk'}, use_global_device_ids=true, to_apply=%add | all-reduce | flops 256 | bytes 2048
  417.7 376.4 %all-gather.5.cloned.1.call-done = bf16[16384,768]{1,0:T(8,128)(2,1)} async-done(((bf16[256,768]{1,0:T(8,128)(2,1)}), bf16[16384,768]{1,0:T(8,128)(2,1)}) %all-gather.5.cloned.1.call-update) | async-done | bytes 25165840 | tf_op jit(solution)/shard_map/all_gather | solution.py:129
  794.0 199.1 %while.16 = (s32[]{:T(128)}, f32[6,260]{1,0:T(8,128)}, f32[6,260]{1,0:T(8,128)}, f32[6,260,128]{2,1,0:T(8,128)}, bf16[16,1024,768]{2,1,0:T(8,128)(2,1)}, /*index...) while((s32[]{:T(128)}, f32[6,260]{1,0:T(8,128)}, f32[6,260]{1,0:T(8,128)}, ...), condition=%wide.region_9.10_spmd, body=%wide.region_6.9_spmd.sunk | while | flops 831071232 | bytes 49750920 | solution.py:86
  794.0 3.2 constant_dynamic-slice_fusion.3
  803.4 2.2 fusion.45
  806.5 3.2 constant_dynamic-slice_fusion.3
  815.8 2.2 fusion.45
  818.9 3.2 constant_dynamic-slice_fusion.3
  828.3 2.2 fusion.45
  831.4 3.2 constant_dynamic-slice_fusion.3
  840.7 2.2 fusion.45
  843.8 3.2 constant_dynamic-slice_fusion.3
  856.3 3.2 constant_dynamic-slice_fusion.3
  868.7 3.2 constant_dynamic-slice_fusion.3
  881.2 3.2 constant_dynamic-slice_fusion.3
  893.6 3.2 constant_dynamic-slice_fusion.3
  906.1 3.2 constant_dynamic-slice_fusion.3
  918.5 3.2 constant_dynamic-slice_fusion.3
  931.0 3.2 constant_dynamic-slice_fusion.3
  943.4 3.2 constant_dynamic-slice_fusion.3
  955.8 3.2 constant_dynamic-slice_fusion.3
  968.3 3.2 constant_dynamic-slice_fusion.3
  980.7 3.2 constant_dynamic-slice_fusion.3
  996.2 40.7 %all-to-all-start.3 = ((bf16[4,64,768]{2,1,0:T(8,128)(2,1)}), bf16[4,64,768]{2,1,0:T(8,128)(2,1)S(1)}, u32[]{:S(2)}, u32[]{:S(2)}) async-start(bf16[4,64,768]{2,1,0:T(8,128)(2,1)} %all_to_all.59), calls=%async_computation.3 | async-start | bytes 786432 | tf_op jit(solution)/shard_map/all_to_all | solution.py:139
  1037.4 9.9 all-to-all-done.3
  (411 shorter events, 153.2 us)
Async XLA Ops:
  7.2 58.0 %copy-start = (f32[128]{0:T(128)S(1)}, f32[128]{0:T(128)}, u32[]{:S(2)}) copy-start(f32[128]{0:T(128)} %param.25) | copy-start | bytes 1540
  7.2 21.6 %copy-start.17 = (s32[64]{0:T(128)S(1)}, s32[64]{0:T(128)}, u32[]{:S(2)}) copy-start(s32[64]{0:T(128)} %param.26) | copy-start | bytes 772
  7.2 21.6 %copy-start.18 = (s32[64]{0:T(128)S(1)}, s32[64]{0:T(128)}, u32[]{:S(2)}) copy-start(s32[64]{0:T(128)} %param.27) | copy-start | bytes 772
  7.2 21.6 %copy-start.19 = (s32[64]{0:T(128)S(1)}, s32[64]{0:T(128)}, u32[]{:S(2)}) copy-start(s32[64]{0:T(128)} %param.28) | copy-start | bytes 772
  7.2 21.6 %copy-start.14 = (f32[128]{0:T(128)S(1)}, f32[128]{0:T(128)}, u32[]{:S(2)}) copy-start(f32[128]{0:T(128)} %param.22) | copy-start | bytes 1540
  7.2 21.7 %copy-start.15 = (f32[128]{0:T(128)S(1)}, f32[128]{0:T(128)}, u32[]{:S(2)}) copy-start(f32[128]{0:T(128)} %param.23) | copy-start | bytes 1540
  7.2 21.9 %copy-start.9 = (bf16[64,3072]{1,0:T(8,128)(2,1)S(1)}, bf16[64,3072]{1,0:T(8,128)(2,1)}, u32[]{:S(2)}) copy-start(bf16[64,3072]{1,0:T(8,128)(2,1)} %param.16) | copy-start | bytes 1179652
  7.2 22.2 %copy-start.10 = (bf16[64,3072]{1,0:T(8,128)(2,1)S(1)}, bf16[64,3072]{1,0:T(8,128)(2,1)}, u32[]{:S(2)}) copy-start(bf16[64,3072]{1,0:T(8,128)(2,1)} %param.17) | copy-start | bytes 1179652
  7.3 410.4 %all-gather.7.cloned.1.call-start = ((), (), s32[]{:S(2)}) async-start(), calls=%async_computation.5 | async-start | bytes 25559040 | tf_op jit(solution)/shard_map/all_gather | solution.py:130
  28.7 765.3 %all-gather.5.cloned.1.call-start = ((), (), s32[]{:S(2)}) async-start(), calls=%async_computation.4 | async-start | bytes 25559040 | tf_op jit(solution)/shard_map/all_gather | solution.py:129
  41.3 23.6 %copy-start.12 = (bf16[4,768]{1,0:T(4,128)(2,1)S(1)}, bf16[4,768]{1,0:T(4,128)(2,1)}, u32[]{:S(2)}) copy-start(bf16[4,768]{1,0:T(4,128)(2,1)} %param.19) | copy-start | bytes 18436
  41.3 23.7 %copy-start.11 = (bf16[4,768]{1,0:T(4,128)(2,1)S(1)}, bf16[4,768]{1,0:T(4,128)(2,1)}, u32[]{:S(2)}) copy-start(bf16[4,768]{1,0:T(4,128)(2,1)} %param.20) | copy-start | bytes 18436
  59.0 178.5 %copy-start.13 = (bf16[4,768]{1,0:T(4,128)(2,1)S(1)}, bf16[4,768]{1,0:T(4,128)(2,1)}, u32[]{:S(2)}) copy-start(bf16[4,768]{1,0:T(4,128)(2,1)} %param.21) | copy-start | bytes 18436
  60.0 341.1 %copy-start.21 = (u32[256]{0:T(256)S(1)}, u32[256]{0:T(256)}, u32[]{:S(2)}) copy-start(u32[256]{0:T(256)} %constant.94) | copy-start | bytes 3076
  60.0 342.3 %copy-start.20 = (s32[4]{0:T(128)S(1)}, s32[4]{0:T(128)}, u32[]{:S(2)}) copy-start(s32[4]{0:T(128)} %param.29) | copy-start | bytes 52
  60.0 353.7 %all-to-all-start = ((bf16[64,4,768]{2,0,1:T(8,128)(2,1)}), bf16[64,4,768]{2,0,1:T(8,128)(2,1)S(1)}, u32[]{:S(2)}, u32[]{:S(2)}) async-start(bf16[64,4,768]{2,0,1:T(8,128)(2,1)} %copy.58), calls=%async_computation | async-start | bytes 786432 | tf_op jit(solution)/shard_map/all_to_all | solution.py:44
  64.9 348.7 %copy-start.16 = (f32[128]{0:T(128)S(1)}, f32[128]{0:T(128)}, u32[]{:S(2)}) copy-start(f32[128]{0:T(128)} %param.24) | copy-start | bytes 1540
  803.2 2.4 copy-start.8
  815.6 2.4 copy-start.8
  828.1 2.4 copy-start.8
  840.5 2.4 copy-start.8
  852.9 2.4 copy-start.8
  865.4 2.4 copy-start.8
  877.8 2.4 copy-start.8
  915.2 2.4 copy-start.8
  927.6 2.4 copy-start.8
  940.1 2.4 copy-start.8
  965.0 2.4 copy-start.8
  977.4 2.4 copy-start.8
  989.9 2.4 copy-start.8
  994.6 53.5 %copy-start.1 = (f32[128]{0:T(128)S(1)}, f32[128]{0:T(128)}, u32[]{:S(2)}) copy-start(f32[128]{0:T(128)} %param.25) | copy-start | bytes 1540
  996.2 51.2 %all-to-all-start.3 = ((bf16[4,64,768]{2,1,0:T(8,128)(2,1)}), bf16[4,64,768]{2,1,0:T(8,128)(2,1)S(1)}, u32[]{:S(2)}, u32[]{:S(2)}) async-start(bf16[4,64,768]{2,1,0:T(8,128)(2,1)} %all_to_all.59), calls=%async_computation.3 | async-start | bytes 786432 | tf_op jit(solution)/shard_map/all_to_all | solution.py:139
  (84 other events, 111.7 us)
Sparse Core Ops, SparseCore 0:
  28.8 376.1 all-gather.6
  406.8 387.2 all-gather.4
where the time goes:
time: 1060 us; the launch traced here: 1050 us
  waiting for transfers between devices  386 us (36%)
  blocking collectives  384 us (36%)
  local copies, waits for them, and re-layouts  131 us (12%)
  matrix products  54.7 us (5%)
  starting transfers between devices  45.7 us (4%)
  other arithmetic  36 us (3%)
  between operations  15.1 us (1%)
    all_gather x1, waiting for transfers between devices, body(): lax.all_gather(group_k, 'blk', axis=0, tiled=True)  376 us
    all_gather x1, blocking collectives, body(): lax.all_gather(norm_tk, 'blk', axis=0, tiled=True)  172 us
    all_gather x1, blocking collectives, body(): lax.all_gather(text_v, 'blk', axis=0, tiled=True)  163 us
    dynamic_slice x48, local copies, waits for them, and re-layouts, absorb(): carry, unused = lax.scan(advance, carry, stacked)  105 us
    all_to_all x1, starting transfers between devices, body(): lax.all_to_all(video_part, 'uly', split_axis=0, concat_axis=1, tiled=True)  40.7 us
    dot_general x17, matrix products, absorb_block(): jnp.einsum('hqk,khd->hqd', expo.astype(jnp.bfloat16), value_heads, prefer...  36.4 us
    reduce_sum x17, other arithmetic, absorb_block(): total = total * factor + jnp.sum(expo, axis=-1)  22.4 us
  transfers between devices with their start and end apart: 4, of which 2 were waited for; matrix products, arithmetic and copies ran while one was open for 2% of the time, Pallas kernels for 0%

commit v1 on v0

v1 whole, which is shorter than its diff:
```python
import functools
import math

import jax
import jax.numpy as jnp
import numpy as np
from jax import lax
from jax.experimental import pallas as pl
from jax.experimental.pallas import tpu as pltpu
from jax.sharding import Mesh
from jax.sharding import PartitionSpec as P

HD = 128
RT = 16
RH = 56
RW = 56
HEADS = 24
GROUPS = 8
PER = HEADS // GROUPS
TOK = 64
TT = 4
KVROWS = 2 * PER * TOK + 32
QROWS = PER * TOK + 16
QT = GROUPS * TOK + 16
OT = QT + 16
BACK = PER * TOK + PER * 16
SCALE = math.log2(math.e) / math.sqrt(HD)
NT = (((1,), (1,)), ((), ()))
Z = ("zh", "zl")
ALL = ("zl", "y", "x", "zh", "c")
VMEM = 56 * 2**20
F32 = jnp.float32
BF16 = jnp.bfloat16


def lane_tables():
    freqs, part = [], []
    for number, width in enumerate((RT, RH, RW)):
        index = np.arange(width // 2, dtype=np.float32)
        freqs.append(np.power(np.float32(256.0), (-2.0 * index / width).astype(np.float32)))
        part.append(np.full((width // 2,), number))
    freqs = np.repeat(np.concatenate(freqs), 2).astype(np.float32)
    part = np.repeat(np.concatenate(part), 2)
    return freqs, part


def rotary_tables(frames, rows_pos, cols_pos):
    freqs, part = lane_tables()
    position = jnp.where(
        part[None, :] == 0,
        frames[:, None],
        jnp.where(part[None, :] == 1, rows_pos[:, None], cols_pos[:, None]),
    )
    angle = position.astype(F32) * freqs[None, :]
    sign = np.where(np.arange(HD) % 2 == 0, -1.0, 1.0).astype(np.float32)
    return jnp.cos(angle), jnp.sin(angle) * sign[None, :]


def norm(values, gain):
    values = values.astype(F32)
    meansq = jnp.mean(values * values, axis=-1, keepdims=True)
    return values * lax.rsqrt(meansq + 1e-06) * gain


def prep_kernel(place, q, k, v, tq, tk, tv, mask, qg, kg, tqg, tkg, cosine, sine, kv_out, q_out):
    even = lax.broadcasted_iota(jnp.int32, (TOK, HD), 1) % 2 == 0
    cos, sin = cosine[...], sine[...]

    def turn(values, gain):
        x = norm(values, gain)
        swapped = jnp.where(even, pltpu.roll(x, HD - 1, 1), pltpu.roll(x, 1, 1))
        return (x * cos + swapped * sin).astype(BF16)

    for head in range(HEADS):
        group, h = divmod(head, PER)
        lanes = slice(head * HD, (head + 1) * HD)
        q_out[group, h * TOK : (h + 1) * TOK, :] = turn(q[:, lanes], qg[...])
        kv_out[group, h * TOK : (h + 1) * TOK, :] = turn(k[:, lanes], kg[...])
        kv_out[group, (PER + h) * TOK : (PER + h + 1) * TOK, :] = v[:, lanes]
    own = place[0]
    zero4 = jnp.zeros((TT, HD), F32)
    tqs, tks, tvs = tq[...].astype(F32), tk[...].astype(F32), tv[...].astype(F32)
    for pair in range(2):
        qrows, krows = [], []
        for h in range(PER):
            at = (pair * PER + h) * HD
            lanes = slice(at, at + HD)
            qrows.append(norm(tqs[:, lanes], tqg[...]))
            krows.append(norm(tks[:, lanes], tkg[...]))
            krows.append(tvs[:, lanes])
        qrows = jnp.concatenate(qrows + [zero4], axis=0)
        krows = jnp.concatenate(krows + [mask[...].astype(F32), zero4], axis=0)
        for group in range(pair, GROUPS, 2):
            mine = own == group // 2
            q_out[group, PER * TOK :, :] = jnp.where(mine, qrows, 0.0).astype(BF16)
            kv_out[group, 2 * PER * TOK :, :] = jnp.where(mine, krows, 0.0).astype(BF16)


def attend_kernel(q, qtext, k, v, text, out, qs, *, block):
    h = pl.program_id(0)
    qs[: GROUPS * TOK, :] = q[...].reshape(GROUPS * TOK, HD)
    rows = qtext[...].astype(F32)
    rows = rows[:4] + rows[4:]
    top = rows[:, :8]
    upper = lax.broadcasted_iota(jnp.int32, (2, 8, HD), 1) < TT

    def pairs(tile, low):
        tile = tile.reshape(2, 2, 8, HD)
        first, second = tile[:, 0], tile[:, 1]
        if low:
            return jnp.where(upper, first, pltpu.roll(second, TT, 1)).reshape(16, HD)
        return jnp.where(upper, pltpu.roll(first, TT, 1), second).reshape(16, HD)

    chosen = jnp.where(h == 0, pairs(top, True), jnp.where(h == 1, pairs(top, False), pairs(rows[:, 8:], True)))
    qs[GROUPS * TOK :, :] = chosen.astype(BF16)
    queries = qs[...]

    both = text[...].astype(F32).reshape(4, 2, 2, 4, 32, HD)
    both = (both[:, 0, 0] + both[:, 0, 1] + both[:, 1, 0] + both[:, 1, 1]).reshape(16, 32, HD)
    tile = jnp.where(h == 0, both[:, :8], jnp.where(h == 1, both[:, 8:16], both[:, 16:24]))
    tkeys = tile.reshape(HD, HD).astype(BF16)
    tvalues = pltpu.roll(tile, TT, 1).reshape(HD, HD).astype(BF16)
    valid = both[:, 24:32].reshape(HD, HD).T[:1, :] > 0.0

    scores = lax.dot_general(queries, tkeys, NT, preferred_element_type=F32) * SCALE
    scores = jnp.where(valid, scores, -1e30)
    largest = jnp.max(scores, axis=1, keepdims=True)
    weights = jnp.where(valid, jnp.exp2(scores - largest), 0.0).astype(BF16)
    ones = jnp.ones((HD, HD), BF16)
    accum = jnp.dot(weights, jnp.concatenate([tvalues, ones], axis=1), preferred_element_type=F32)
    ones = jnp.ones((block, HD), BF16)
    step = block // TOK
    for at in range(0, k.shape[0], step):
        keys = k[at : at + step].reshape(block, HD)
        values = v[at : at + step].reshape(block, HD)
        scores = lax.dot_general(queries, keys, NT, preferred_element_type=F32) * SCALE
        newest = jnp.maximum(largest, jnp.max(scores, axis=1, keepdims=True))
        weights = jnp.exp2(scores - newest).astype(BF16)
        mixed = jnp.dot(weights, jnp.concatenate([values, ones], axis=1), preferred_element_type=F32)
        accum = accum * jnp.exp2(largest - newest) + mixed
        largest = newest
    total = accum[:, HD:]
    out[0, :QT, :] = (accum[:, :HD] / total).astype(BF16)
    logs = largest + jnp.log2(total)
    logs = jnp.concatenate([logs, jnp.zeros((5 * HD - QT, HD), F32)], axis=0).T[:1, :]
    logs = jnp.concatenate([logs[:, i * HD : (i + 1) * HD] for i in range(5)], axis=0)
    high = logs.astype(BF16).astype(F32)
    middle = (logs - high).astype(BF16).astype(F32)
    low = logs - high - middle
    out[0, QT:, :] = jnp.concatenate([high, middle, low, jnp.zeros((1, HD), F32)], axis=0).astype(BF16)


def combine_kernel(parts, out):
    logs = []
    for s in range(4):
        pieces = parts[s, 0, QT:, :].astype(F32)
        logs.append(pieces[0:5] + pieces[5:10] + pieces[10:15])
    top = functools.reduce(jnp.maximum, logs)
    shares = [jnp.exp2(l - top) for l in logs]
    total = sum(shares)
    shares = [s / total for s in shares]

    def spread(share):
        row = jnp.concatenate([share[i : i + 1] for i in range(5)], axis=1)
        return jnp.broadcast_to(row, (HD, 5 * HD)).T[:QT]

    mixed = sum(spread(shares[s]) * parts[s, 0, :QT, :].astype(F32) for s in range(4)).astype(BF16)
    h = pl.program_id(0)
    video = mixed[: GROUPS * TOK].reshape(GROUPS, TOK, HD)
    text = jnp.broadcast_to(mixed[GROUPS * TOK :][None], (GROUPS, 16, HD))
    for i in range(PER):

        @pl.when(h == i)
        def _():
            out[:, i * TOK : (i + 1) * TOK, :] = video
            out[:, PER * TOK + i * 16 : PER * TOK + (i + 1) * 16, :] = text


def final_kernel(place, parts, video, text):
    for head in range(HEADS):
        group, h = divmod(head, PER)
        video[:, head * HD : (head + 1) * HD] = parts[group, h * TOK : (h + 1) * TOK, :]
    own, zl = place[0], place[1]
    rows = lax.broadcasted_iota(jnp.int32, (8, 16), 0)
    columns = lax.broadcasted_iota(jnp.int32, (8, 16), 1)
    pick = (columns == rows + TT * zl).astype(F32).astype(BF16)
    for pair in range(2):
        for h in range(PER):
            at = PER * TOK + h * 16
            piece = jnp.zeros((16, HD), F32)
            for u in range(4):
                piece += jnp.where(own == u, parts[2 * u + pair, at : at + 16, :].astype(F32), 0.0)
            chosen = jnp.dot(pick, piece.astype(BF16), preferred_element_type=F32)
            lanes = (pair * PER + h) * HD
            text[:, lanes : lanes + HD] = chosen[:TT].astype(BF16)


def whole(*shapes):
    return [pl.BlockSpec(memory_space=pltpu.VMEM) for _ in shapes]


def body(
    video_q,
    video_k,
    video_v,
    text_q,
    text_k,
    text_v,
    video_q_gain,
    video_k_gain,
    text_q_gain,
    text_k_gain,
    frame_ids,
    row_ids,
    col_ids,
    text_mask,
):
    own = 2 * lax.axis_index("zh") + lax.axis_index("c")
    place = jnp.stack([own, lax.axis_index("zl")]).astype(jnp.int32)
    params = pltpu.CompilerParams(vmem_limit_bytes=VMEM)
    cosine, sine = rotary_tables(frame_ids, row_ids, col_ids)
    mask = jnp.broadcast_to(text_mask[:, None], (TT, HD))
    gains = [g.reshape(1, HD) for g in (video_q_gain, video_k_gain, text_q_gain, text_k_gain)]
    operands = (video_q, video_k, video_v, text_q, text_k, text_v, mask, *gains, cosine, sine)
    kv, q = pl.pallas_call(
        prep_kernel,
        out_shape=(
            jax.ShapeDtypeStruct((GROUPS, KVROWS, HD), BF16),
            jax.ShapeDtypeStruct((GROUPS, QROWS, HD), BF16),
        ),
        in_specs=[pl.BlockSpec(memory_space=pltpu.SMEM)] + whole(*operands),
        out_specs=tuple(whole(0, 0)),
        compiler_params=params,
        name="prep",
    )(place, *operands)
    kv = lax.all_to_all(kv, Z, split_axis=0, concat_axis=0, tiled=True)
    q = lax.all_to_all(q, Z, split_axis=0, concat_axis=0, tiled=True)
    kv = lax.all_gather(kv, ("y", "c"), axis=0, tiled=True)
    q = lax.all_gather(q, "x", axis=0, tiled=True)
    sources = kv.shape[0]
    parts = pl.pallas_call(
        functools.partial(attend_kernel, block=1024),
        grid=(PER, 4),
        in_specs=[
            pl.BlockSpec((GROUPS, TOK, HD), lambda h, x: (x, h, 0)),
            pl.BlockSpec((GROUPS, 16, HD), lambda h, x: (x, PER * TOK // 16, 0)),
            pl.BlockSpec((sources, TOK, HD), lambda h, x: (0, h, 0)),
            pl.BlockSpec((sources, TOK, HD), lambda h, x: (0, PER + h, 0)),
            pl.BlockSpec((sources, 32, HD), lambda h, x: (0, 2 * PER * TOK // 32, 0)),
        ],
        out_specs=pl.BlockSpec((1, OT, HD), lambda h, x: (x, h, 0)),
        out_shape=jax.ShapeDtypeStruct((4, PER * OT, HD), BF16),
        scratch_shapes=[pltpu.VMEM((QT, HD), BF16)],
        compiler_params=params,
        name="attend",
    )(q, q, kv, kv, kv)
    parts = lax.all_to_all(parts, "x", split_axis=0, concat_axis=0, tiled=True)
    back = pl.pallas_call(
        combine_kernel,
        grid=(PER,),
        in_specs=[pl.BlockSpec((4, 1, OT, HD), lambda h: (0, h, 0, 0))],
        out_specs=pl.BlockSpec((GROUPS, BACK, HD), lambda h: (0, 0, 0)),
        out_shape=jax.ShapeDtypeStruct((GROUPS, BACK, HD), BF16),
        compiler_params=params,
        name="combine",
    )(parts.reshape(4, PER, OT, HD))
    back = lax.all_to_all(back, Z, split_axis=0, concat_axis=0, tiled=True)
    return pl.pallas_call(
        final_kernel,
        out_shape=(
            jax.ShapeDtypeStruct(video_q.shape, BF16),
            jax.ShapeDtypeStruct(text_q.shape, BF16),
        ),
        in_specs=[pl.BlockSpec(memory_space=pltpu.SMEM)] + whole(0),
        out_specs=tuple(whole(0, 0)),
        compiler_params=params,
        name="final",
    )(place, back)


def solution(mesh):
    devices = mesh.devices.reshape(4, 4, 4, 2, 2)
    mesh = Mesh(devices, ALL)
    tokens = P(ALL, None)
    text = P(("zl", "y", "x"), ("zh", "c"))
    ids = P(ALL)
    in_specs = (tokens, tokens, tokens, text, text, text, P(), P(), P(), P(), ids, ids, ids, P(("zl", "y", "x")))
    out_specs = (tokens, text)
    return jax.shard_map(body, mesh=mesh, in_specs=in_specs, out_specs=out_specs, check_vma=False)
```

time: 1060 us -> 223 us (0.21)
  waiting for transfers between devices: 386 us -> 51.8 us
  blocking collectives: 384 us -> 95.3 us
  local copies, waits for them, and re-layouts: 131 us -> 1.3 us
  Pallas kernels: 0 us -> 57.4 us
  matrix products: 54.7 us -> 0 us
  starting transfers between devices: 45.7 us -> 0.08 us
  other arithmetic: 36 us -> 2.21 us
    all_gather x2 -> x0, blocking collectives: 335 us -> none  [the longest x1 172 us: body(): lax.all_gather(norm_tk, 'blk', axis=0, tiled=True)]
    all_gather x2, waiting for transfers between devices: 376 us -> 51.8 us  [the longest x1 48 us: body(): kv = lax.all_gather(kv, ('y', 'c'), axis=0, tiled=True)]
    dynamic_slice x48 -> x0, local copies, waits for them, and re-layouts: 105 us -> none  [absorb(): carry, unused = lax.scan(advance, carry, stacked)]
    all_to_all x2 -> x4, blocking collectives: 37.9 us -> 95.3 us  [the longest x1 26 us: body(): parts = lax.all_to_all(parts, 'x', split_axis=0, concat_axis=0, tiled=True)]
    pallas_call x0 -> x4, Pallas kernels: none -> 57.4 us  [the longest x1 43.7 us: body(): pl.pallas_call(functools.partial(attend_kernel, block=1024), grid=(PER, 4...]
    dot_general x34 -> x0, matrix products: 54.7 us -> none  [the longest x17 36.4 us: absorb_block(): jnp.einsum('hqk,khd->hqd', expo.astype(jnp.bfloat16), value_heads, prefer...]
    all_to_all x2 -> x0, starting transfers between devices: 45.6 us -> none  [the longest x1 40.7 us: body(): lax.all_to_all(video_part, 'uly', split_axis=0, concat_axis=1, tiled=True)]
    reduce_sum x21 -> x0, other arithmetic: 22.8 us -> none  [the longest x17 22.4 us: absorb_block(): total = total * factor + jnp.sum(expo, axis=-1)]
  transfers between devices with their start and end apart: 4 -> 2, of which waited for: 2 -> 2; matrix products, arithmetic and copies ran while one was open for 2% -> 0% of each run, Pallas kernels for 0% -> 0%
where the time goes in v1:
time: 223 us; the launch traced here: 222 us
  blocking collectives  95.3 us (43%)
  Pallas kernels  57.4 us (26%)
  waiting for transfers between devices  51.8 us (23%)
  between operations  14.1 us (6%)
    all_gather x1, waiting for transfers between devices, body(): kv = lax.all_gather(kv, ('y', 'c'), axis=0, tiled=True)  48 us
    pallas_call x1, Pallas kernels, body(): pl.pallas_call(functools.partial(attend_kernel, block=1024), grid=(PER, 4...  43.7 us
    all_to_all x1, blocking collectives, body(): parts = lax.all_to_all(parts, 'x', split_axis=0, concat_axis=0, tiled=True)  26 us
    all_to_all x1, blocking collectives, body(): kv = lax.all_to_all(kv, Z, split_axis=0, concat_axis=0, tiled=True)  24.5 us
    all_to_all x1, blocking collectives, body(): q = lax.all_to_all(q, Z, split_axis=0, concat_axis=0, tiled=True)  23.1 us
    all_to_all x1, blocking collectives, body(): back = lax.all_to_all(back, Z, split_axis=0, concat_axis=0, tiled=True)  21.6 us
    pallas_call x1, Pallas kernels, body(): pl.pallas_call(prep_kernel, out_shape=(jax.ShapeDtypeStruct((GROUPS, KVRO...  8.06 us
  transfers between devices with their start and end apart: 2, of which 2 were waited for; matrix products, arithmetic and copies ran while one was open for 0% of the time, Pallas kernels for 0%

profile of v1, /device:TPU:1, one launch (start us, length us, event | category | flops | bytes accessed | tf_op | source)
XLA Modules:
  0.0 222.2 jit_solution(1078792138163190388)
XLA Ops:
  7.2 0.0 all-gather.3.cloned.1.call-start
  7.2 0.6 pad_add_fusion.place
  7.8 1.6 sine_multiply_fusion
  9.4 1.3 broadcast_in_dim.53.mask
  10.7 8.1 %prep.1 = (bf16[8,416,128]{2,1,0:T(8,128)(2,1)}, bf16[8,208,128]{2,1,0:T(8,128)(2,1)}) custom-call(s32[2]{0:T(128)} %pad_add_fusion.place, bf16[64,3072]{1,0:T(8,128)(2,1)} %q.1, bf16[64,3072]{1,0:T(8,128)(2,1)} %k.1, bf16[64,3072]{1,0:T(8,128)(2,1)} %v.1, bf16[4,768]{1,0:T(4,128)(2,1)} %tq.1, bf16[4,768]{1,0:T(4,128)(2,1)} %tk.1, bf16[4,768]{1,0:T(4,128)(2,1)} %tv.1, ...), custom_call_target="tpu_custom_call" | custom-call | tf_op jit(solution)/shard_map/prep/pallas_call | solution.py:225
  18.8 0.0 copy-start
  18.8 23.1 %all_to_all.20 = bf16[8,208,128]{2,1,0:T(8,128)(2,1)} all-to-all(bf16[8,208,128]{2,1,0:T(8,128)(2,1)} %get-tuple-element.4), channel_id=1, replica_groups=mesh['zl'=4,'y'=4,'x'=4,'zh'=2,'c'=2] {'zh','zl'}, dimensions={0} | all-to-all | bytes 851968 | tf_op jit(solution)/shard_map/all_to_all | solution.py:237
  41.9 0.0 all-gather.3.cloned.1.call-update
  41.9 0.0 all-gather.5.cloned.1.call-start
  42.0 0.0 copy-done
  42.0 24.5 %all_to_all.21 = bf16[8,416,128]{2,1,0:T(8,128)(2,1)} all-to-all(bf16[8,416,128]{2,1,0:T(8,128)(2,1)S(1)} %copy-done), channel_id=1, replica_groups=mesh['zl'=4,'y'=4,'x'=4,'zh'=2,'c'=2] {'zh','zl'}, dimensions={0} | all-to-all | bytes 1703936 | tf_op jit(solution)/shard_map/all_to_all | solution.py:236
  66.5 0.0 all-gather.5.cloned.1.call-update
  66.5 3.8 %all-gather.3.cloned.1.call-done.q.qtext = bf16[32,208,128]{2,1,0:T(8,128)(2,1)} async-done(((bf16[8,208,128]{2,1,0:T(8,128)(2,1)}), bf16[32,208,128]{2,1,0:T(8,128)(2,1)}) %all-gather.3.cloned.1.call-update) | async-done | bytes 1703952 | tf_op jit(solution)/shard_map/all_gather | solution.py:239
  70.4 48.0 %all-gather.5.cloned.1.call-done.k.v.text = bf16[64,416,128]{2,1,0:T(8,128)(2,1)} async-done(((bf16[8,416,128]{2,1,0:T(8,128)(2,1)}), bf16[64,416,128]{2,1,0:T(8,128)(2,1)}) %all-gather.5.cloned.1.call-update) | async-done | bytes 6815760 | tf_op jit(solution)/shard_map/all_gather | solution.py:238
  118.3 43.7 %attend.1 = bf16[4,1632,128]{2,1,0:T(8,128)(2,1)} custom-call(bf16[32,208,128]{2,1,0:T(8,128)(2,1)} %all-gather.3.cloned.1.call-done.q.qtext, bf16[32,208,128]{2,1,0:T(8,128)(2,1)} %all-gather.3.cloned.1.call-done.q.qtext, bf16[64,416,128]{2,1,0:T(8,128)(2,1)} %all-gather.5.cloned.1.call-done.k.v.text, ...), custom_call_target="tpu_custom_call" | custom-call | tf_op jit(solution)/shard_map/attend/pallas_call | solution.py:241
  162.0 26.0 %all_to_all.22 = bf16[4,1632,128]{2,1,0:T(8,128)(2,1)} all-to-all(bf16[4,1632,128]{2,1,0:T(8,128)(2,1)} %attend.1), channel_id=1, replica_groups=mesh['zl'=4,'y'=4,'x'=4,'zh'=2,'c'=2] {'x'}, dimensions={0} | all-to-all | bytes 3342336 | tf_op jit(solution)/shard_map/all_to_all | solution.py:257
  188.0 3.8 %combine.1 = bf16[8,240,128]{2,1,0:T(8,128)(2,1)} custom-call(bf16[4,3,544,128]{3,2,1,0:T(8,128)(2,1)} %bitcast.7), custom_call_target="tpu_custom_call" | custom-call | tf_op jit(solution)/shard_map/combine/pallas_call | solution.py:258
  191.8 21.6 %all_to_all.23.parts = bf16[8,240,128]{2,1,0:T(8,128)(2,1)} all-to-all(bf16[8,240,128]{2,1,0:T(8,128)(2,1)} %combine.1), channel_id=1, replica_groups=mesh['zl'=4,'y'=4,'x'=4,'zh'=2,'c'=2] {'zh','zl'}, dimensions={0} | all-to-all | bytes 983040 | tf_op jit(solution)/shard_map/all_to_all | solution.py:267
  213.5 1.9 final.1
Async XLA Ops:
  7.2 63.2 %all-gather.3.cloned.1.call-start = ((), (), s32[]{:S(2)}) async-start(), calls=%async_computation.4 | async-start | bytes 2129920 | tf_op jit(solution)/shard_map/all_gather | solution.py:239
  18.8 23.2 %copy-start = (bf16[8,416,128]{2,1,0:T(8,128)(2,1)S(1)}, bf16[8,416,128]{2,1,0:T(8,128)(2,1)}, u32[]{:S(2)}) copy-start(bf16[8,416,128]{2,1,0:T(8,128)(2,1)} %get-tuple-element.5) | copy-start | bytes 2555908
  41.9 76.4 %all-gather.5.cloned.1.call-start = ((), (), s32[]{:S(2)}) async-start(), calls=%async_computation.5 | async-start | bytes 7667712 | tf_op jit(solution)/shard_map/all_gather | solution.py:238
Sparse Core Ops, SparseCore 0:
  42.0 28.2 all-gather.2
  72.2 46.0 all-gather.4
